TPU v7x, 512 devices: a whole 4x4x16 slice. The times are simulated.
512 devices in a mesh: row: 16 (over z_hi, x), col: 8 (over z_lo, core), layer: 4 (over y).
Axes of the slice: x: 4, y: 4, z: 16 (z_hi: 4, z_lo: 4; z = z_hi * 4 + z_lo), core: 2. Of those that a mesh axis runs over, the one named last changes fastest.
Arguments:
- blocks: bfloat16 [2048, 128, 128], P(('row', 'col')), may hold values from -2 to 2
- left_pick: int32 [2048], P(('row', 'col', 'layer')), may hold values from 0 to 15, as said below
- right_pick: int32 [2048], P(('row', 'col', 'layer')), may hold values from 0 to 15, as said below
- term_left: int32 [8192, 24], P(('row', 'col', 'layer')), may hold values from 0 to 31
- term_right: int32 [8192, 24], P(('row', 'col', 'layer')), may hold values from 0 to 63
- term_count: int32 [8192], P(('row', 'col', 'layer')), may hold values from 1 to 24
Outputs:
- product: float32 [2048, 128, 128], P(('row', 'col', 'layer'))
Inputs may be any that keep to these rules, and one draw needn't show every extreme that they name: `left_pick`: for each tile, the 4 lists of 4 slots together name each of the tile's 16 slots exactly once. `right_pick`: for each tile, the 4 lists of 4 slots together name each of the tile's 16 slots exactly once.
All inputs are finite; a program needn't handle non-finite values.
Results may differ from a plain program's by a relative error of at most 0.0003.
Values may be sent and summed in bfloat16 or wider, within the bound.
A program may use at most 64 MiB of HBM per device.

v0:
```python
import jax
import jax.numpy as jnp
from jax import lax
from jax.sharding import PartitionSpec as P


def shards(blocks, left_pick, right_pick, term_left, term_right, term_count):
    slots = blocks.shape[0]
    width = blocks.shape[1]
    picks = left_pick.shape[0]
    terms = term_left.shape[1]
    row_blocks = lax.all_gather(blocks, "col", axis=0, tiled=True)
    row_lists = lax.all_gather(left_pick, "col", axis=0, tiled=True)
    col_blocks = lax.all_gather(blocks, "row", axis=0, tiled=True)
    col_lists = lax.all_gather(right_pick, "row", axis=0, tiled=True)
    left_owner = jnp.arange(row_lists.shape[0], dtype=jnp.int32) // picks
    right_owner = jnp.arange(col_lists.shape[0], dtype=jnp.int32) // picks
    left_index = (left_owner * slots + row_lists)[term_left]
    right_index = (right_owner * slots + col_lists)[term_right]
    live = jnp.arange(terms, dtype=jnp.int32)[None, :] < term_count[:, None]
    groups = slots // 4

    def one_group(inputs):
        left_ids, right_ids, live_now = inputs
        left_sel = jnp.where(
            live_now[:, :, None, None], row_blocks[left_ids], jnp.zeros((), jnp.bfloat16)
        )
        right_sel = col_blocks[right_ids]
        return lax.dot_general(
            left_sel,
            right_sel,
            (((1, 3), (1, 2)), ((0,), (0,))),
            preferred_element_type=jnp.float32,
        )

    partial_sums = lax.map(
        one_group,
        (
            left_index.reshape(groups, 4, terms),
            right_index.reshape(groups, 4, terms),
            live.reshape(groups, 4, terms),
        ),
    )
    partial_sums = partial_sums.reshape(slots, width, width)
    return lax.psum_scatter(partial_sums, "layer", scatter_dimension=0, tiled=True)


def solution(mesh):
    in_specs = (
        P(("row", "col"), None, None),
        P(("row", "col", "layer")),
        P(("row", "col", "layer")),
        P(("row", "col", "layer"), None),
        P(("row", "col", "layer"), None),
        P(("row", "col", "layer")),
    )
    out_specs = P(("row", "col", "layer"), None, None)
    return jax.shard_map(shards, mesh=mesh, in_specs=in_specs, out_specs=out_specs, check_vma=False)
```

profile of v0, /device:TPU:1, one launch (start us, length us, event | category | flops | bytes accessed | tf_op | source)
XLA Modules:
  0.0 378.1 jit_solution(7717388862422169837)
XLA Ops:
  6.5 0.7 all-gather.3.cloned.1.call-update
  7.3 0.0 all-gather.5.cloned.1.call-start
  7.3 0.7 all-gather.5.cloned.1.call-update
  8.0 0.0 reduce-scatter.2.cloned.1.call-start
  8.1 0.7 compare_select_fusion.3
  8.8 0.1 reshape.98
  8.9 1.2 dynamic-slice
  10.7 0.9 dynamic-update-slice
  11.5 9.5 %all-reduce = s32[32]{0:T(128)S(1)} all-reduce(s32[32]{0:T(128)S(1)} %dynamic-update-slice), channel_id=1, replica_groups=mesh['row'=16,'col'=8,'layer'=4] {'col'}, use_global_device_ids=true, to_apply=%add | all-reduce | flops 32 | bytes 256
  21.0 0.0 copy-start
  21.0 0.0 copy-start.2
  21.0 2.7 gather_fusion.2
  23.7 0.1 reshape.77
  23.8 1.2 dynamic-slice.1
  25.6 0.0 copy-done
  25.6 0.1 reshape.106
  25.7 0.2 dynamic-update-slice.1
  26.0 22.2 %all-reduce.1 = s32[64]{0:T(128)S(1)} all-reduce(s32[64]{0:T(128)S(1)} %dynamic-update-slice.1), channel_id=1, replica_groups=mesh['row'=16,'col'=8,'layer'=4] {'row'}, use_global_device_ids=true, to_apply=%add.1 | all-reduce | flops 64 | bytes 512
  48.2 0.0 copy-start.1
  48.2 2.7 gather_fusion.3
  50.9 0.1 reshape.78
  51.0 0.1 lt.46
  51.1 0.1 iota_compare_fusion
  51.2 21.3 %all-gather.3.cloned.1.call-done = bf16[128,128,128]{2,1,0:T(8,128)(2,1)} async-done(((bf16[16,128,128]{2,1,0:T(8,128)(2,1)}), bf16[128,128,128]{2,1,0:T(8,128)(2,1)}) %all-gather.3.cloned.1.call-update) | async-done | bytes 4194320 | tf_op jit(solution)/shard_map/all_gather | solution.py:12
  72.5 220.2 %all-gather.5.cloned.1.call-done = bf16[256,128,128]{2,1,0:T(8,128)(2,1)} async-done(((bf16[16,128,128]{2,1,0:T(8,128)(2,1)}), bf16[256,128,128]{2,1,0:T(8,128)(2,1)}) %all-gather.5.cloned.1.call-update) | async-done | bytes 8388624 | tf_op jit(solution)/shard_map/all_gather | solution.py:14
  292.7 52.9 %while.10 = (s32[]{:T(128)}, f32[4,4,128,128]{3,2,1,0:T(8,128)}, pred[4,4,24]{2,1,0:T(4,128)(4,1)S(1)}, s32[4,4,24]{2,1,0:T(4,128)S(1)}, bf16[128,128,128]{2,1,0...) while((s32[]{:T(128)}, f32[4,4,128,128]{3,2,1,0:T(8,128)}, ...), condition=%wide.region_1.2_spmd, body=%wide.region_0.1_spmd.sunk | while | flops 404228672 | bytes 19150204 | solution.py:36
  292.7 0.1 reshape.141
  292.8 4.5 %gather_fusion = bf16[96,128,128]{2,1,0:T(8,128)(2,1)S(1)} fusion(bf16[256,128,128]{2,1,0:T(8,128)(2,1)} %get-tuple-element.128, s32[1024]{0:T(1024)S(1)} %pad_clamp_fusion.6), kind=kCustom, calls=%fused_computation.1.clone.1 | custom fusion | bytes 6291840 | tf_op jit(solution)/shard_map/while/body/eval_jaxpr/gather | solution.py:28
  297.3 0.1 reshape.142
  297.4 4.9 %gather_fusion.1 = bf16[96,128,128]{2,1,0:T(8,128)(2,1)} fusion(bf16[128,128,128]{2,1,0:T(8,128)(2,1)} %get-tuple-element.126, s32[1024]{0:T(1024)S(1)} %pad_clamp_fusion.7), kind=kCustom, calls=%fused_computation.clone.1 | custom fusion | bytes 6291840 | tf_op jit(solution)/shard_map/while/body/eval_jaxpr/gather | solution.py:26
  302.3 3.6 fusion.21
  305.9 0.1 reshape.141
  306.0 4.5 %gather_fusion = bf16[96,128,128]{2,1,0:T(8,128)(2,1)S(1)} fusion(bf16[256,128,128]{2,1,0:T(8,128)(2,1)} %get-tuple-element.128, s32[1024]{0:T(1024)S(1)} %pad_clamp_fusion.6), kind=kCustom, calls=%fused_computation.1.clone.1 | custom fusion | bytes 6291840 | tf_op jit(solution)/shard_map/while/body/eval_jaxpr/gather | solution.py:28
  310.6 0.1 reshape.142
  310.7 4.9 %gather_fusion.1 = bf16[96,128,128]{2,1,0:T(8,128)(2,1)} fusion(bf16[128,128,128]{2,1,0:T(8,128)(2,1)} %get-tuple-element.126, s32[1024]{0:T(1024)S(1)} %pad_clamp_fusion.7), kind=kCustom, calls=%fused_computation.clone.1 | custom fusion | bytes 6291840 | tf_op jit(solution)/shard_map/while/body/eval_jaxpr/gather | solution.py:26
  315.5 3.6 fusion.21
  319.1 0.1 reshape.141
  319.2 4.5 %gather_fusion = bf16[96,128,128]{2,1,0:T(8,128)(2,1)S(1)} fusion(bf16[256,128,128]{2,1,0:T(8,128)(2,1)} %get-tuple-element.128, s32[1024]{0:T(1024)S(1)} %pad_clamp_fusion.6), kind=kCustom, calls=%fused_computation.1.clone.1 | custom fusion | bytes 6291840 | tf_op jit(solution)/shard_map/while/body/eval_jaxpr/gather | solution.py:28
  323.8 0.1 reshape.142
  323.9 4.9 %gather_fusion.1 = bf16[96,128,128]{2,1,0:T(8,128)(2,1)} fusion(bf16[128,128,128]{2,1,0:T(8,128)(2,1)} %get-tuple-element.126, s32[1024]{0:T(1024)S(1)} %pad_clamp_fusion.7), kind=kCustom, calls=%fused_computation.clone.1 | custom fusion | bytes 6291840 | tf_op jit(solution)/shard_map/while/body/eval_jaxpr/gather | solution.py:26
  328.8 3.6 fusion.21
  332.4 0.1 reshape.141
  332.5 4.5 %gather_fusion = bf16[96,128,128]{2,1,0:T(8,128)(2,1)S(1)} fusion(bf16[256,128,128]{2,1,0:T(8,128)(2,1)} %get-tuple-element.128, s32[1024]{0:T(1024)S(1)} %pad_clamp_fusion.6), kind=kCustom, calls=%fused_computation.1.clone.1 | custom fusion | bytes 6291840 | tf_op jit(solution)/shard_map/while/body/eval_jaxpr/gather | solution.py:28
  337.0 0.1 reshape.142
  337.1 4.9 %gather_fusion.1 = bf16[96,128,128]{2,1,0:T(8,128)(2,1)} fusion(bf16[128,128,128]{2,1,0:T(8,128)(2,1)} %get-tuple-element.126, s32[1024]{0:T(1024)S(1)} %pad_clamp_fusion.7), kind=kCustom, calls=%fused_computation.clone.1 | custom fusion | bytes 6291840 | tf_op jit(solution)/shard_map/while/body/eval_jaxpr/gather | solution.py:26
  342.0 3.6 fusion.21
  345.6 0.0 reduce-scatter.2.cloned.1.call-update
  345.6 26.0 %reduce-scatter.2.cloned.1.call-done = f32[4,128,128]{2,1,0:T(8,128)} async-done(((f32[16,128,128]{2,1,0:T(8,128)}), f32[4,128,128]{2,1,0:T(8,128)}) %reduce-scatter.2.cloned.1.call-update) | async-done | bytes 262160 | tf_op jit(solution)/shard_map/reduce_scatter | solution.py:45
  (27 shorter events, 0.1 us)
Async XLA Ops:
  6.5 66.0 %all-gather.3.cloned.1.call-start = ((), (), s32[]{:S(2)}) async-start(), calls=%async_computation.1 | async-start | bytes 4718592 | tf_op jit(solution)/shard_map/all_gather | solution.py:12
  7.3 285.4 %all-gather.5.cloned.1.call-start = ((), (), s32[]{:S(2)}) async-start(), calls=%async_computation.2 | async-start | bytes 8912896 | tf_op jit(solution)/shard_map/all_gather | solution.py:14
  8.0 363.6 %reduce-scatter.2.cloned.1.call-start = ((), (), s32[]{:S(2)}) async-start(), calls=%async_computation.3 | async-start | bytes 1310720 | tf_op jit(solution)/shard_map/reduce_scatter | solution.py:45
  21.0 4.6 %copy-start = (s32[16,24]{1,0:T(8,128)S(1)}, s32[16,24]{1,0:T(8,128)}, u32[]{:S(2)}) copy-start(s32[16,24]{1,0:T(8,128)} %param.12) | copy-start | bytes 4612
  21.0 4.7 %copy-start.2 = (s32[4]{0:T(128)S(1)}, s32[4]{0:T(128)}, u32[]{:S(2)}) copy-start(s32[4]{0:T(128)} %param.10) | copy-start | bytes 52
  48.2 2.8 copy-start.1
Sparse Core Ops, SparseCore 0:
  9.4 63.0 all-gather.2
  75.5 217.1 all-gather.4
  345.8 25.7 reduce-scatter.1
where the time goes:
time: 379 us; the launch traced here: 378 us
  waiting for transfers between devices  269 us (71%)
  local copies, waits for them, and re-layouts  47.7 us (13%)
  blocking collectives  31.7 us (8%)
  matrix products  14.5 us (4%)
  between operations  14.3 us (4%)
    all_gather x1, waiting for transfers between devices, shards(): col_blocks = lax.all_gather(blocks, 'row', axis=0, tiled=True)  220 us
    unnamed x2, blocking collectives  31.7 us
    reduce_scatter x1, waiting for transfers between devices, shards(): lax.psum_scatter(partial_sums, 'layer', scatter_dimension=0, tiled=True)  26 us
    all_gather x1, waiting for transfers between devices, shards(): row_blocks = lax.all_gather(blocks, 'col', axis=0, tiled=True)  21.3 us
    gather x4, local copies, waits for them, and re-layouts, one_group(): row_blocks[left_ids]  19.5 us
    gather x4, local copies, waits for them, and re-layouts, one_group(): right_sel = col_blocks[right_ids]  18.1 us
    dot_general x4, matrix products, one_group(): lax.dot_general(left_sel, right_sel, (((1, 3), (1, 2)), ((0,), (0,))), pr...  14.5 us
  transfers between devices with their start and end apart: 3, of which 3 were waited for; matrix products, arithmetic and copies ran while one was open for 3% of the time, Pallas kernels for 0%

commit v1 on v0

v1 whole, which is shorter than its diff:
```python
import functools

import jax
import jax.numpy as jnp
from jax import lax
from jax.experimental import pallas as pl
from jax.experimental.pallas import tpu as pltpu
from jax.sharding import PartitionSpec as P

MESH = pl.DeviceIdType.MESH
BS = 128
PICK = 4
SLOTS = 16
TERMS = 24
N_ROW = 16
N_COL = 8
N_LAYER = 4
N_LEFT = N_COL * PICK
N_RIGHT = N_ROW * PICK


def kernel(
    blocks,
    left_pick,
    right_pick,
    term_left,
    term_right,
    term_count,
    out,
    left,
    right,
    part,
    from_down,
    from_up,
    last_down,
    last_up,
    z_send,
    z_recv,
    x_send,
    x_recv,
    l_send,
    l_recv,
    c_send,
    c_recv,
    y_send,
    y_recv,
):
    row = lax.axis_index("row")
    col = lax.axis_index("col")
    layer = lax.axis_index("layer")
    z_hi, x = row // 4, row % 4
    z_lo, core = col // 2, col % 2

    def at_z(step):
        return (((z_hi + step) % 4) * 4 + x, col, layer)

    def at_x(step):
        return (z_hi * 4 + (x + step) % 4, col, layer)

    def at_line(step):
        return (row, ((z_lo + step) % 4) * 2 + core, layer)

    def at_y(step):
        return (row, col, (layer + step) % 4)

    sibling = (row, z_lo * 2 + 1 - core, layer)

    barrier = pltpu.get_barrier_semaphore()
    partners = [at_z(1), at_z(3), at_x(1), at_x(3), at_line(1), at_line(2), at_line(3), sibling, at_y(1), at_y(3)]
    for partner in partners:
        pl.semaphore_signal(barrier, inc=1, device_id=partner, device_id_type=MESH)
    for j in range(PICK):
        right[row * PICK + j] = blocks[right_pick[j]]
    for j in range(PICK):
        left[col * PICK + j] = blocks[left_pick[j]]
    left[N_LEFT] = jnp.zeros((BS, BS), jnp.bfloat16)
    pl.semaphore_wait(barrier, len(partners))

    def copy(ref, first, count, send, recv, target):
        return pltpu.make_async_remote_copy(
            src_ref=ref.at[pl.ds(first, count)],
            dst_ref=ref.at[pl.ds(first, count)],
            send_sem=send,
            recv_sem=recv,
            device_id=target,
            device_id_type=MESH,
        )

    def first_of(h, xx, half):
        return (((h + 4) % 4) * 4 + (xx + 4) % 4) * PICK + 2 * half

    def z_copy(h, half, step, k):
        return copy(right, first_of(h, x, half), 2, z_send.at[k], z_recv.at[k], at_z(step))

    def x_copy(dz, half, step, xx):
        k = (dz * 2 + half) * 2 + (0 if step == 1 else 1)
        return copy(right, first_of(z_hi + dz, xx, half), 2, x_send.at[k], x_recv.at[k], at_x(step))

    def x_forward(dz, half, step, xx):
        k = 16 + (dz * 2 + half) * 2 + (0 if step == 1 else 1)
        piece = 0 if step == 1 else 1
        return copy(right, first_of(z_hi + dz, xx, half) + piece, 1, x_send.at[k], x_recv.at[k], at_x(step))

    def x_start(dz, half):
        x_copy(dz, half, 1, x).start()
        x_copy(dz, half, 3, x).start()

    def x_pass(dz, half):
        x_copy(dz, half, 1, x - 1).wait_recv()
        x_forward(dz, half, 1, x - 1).start()
        x_copy(dz, half, 3, x + 1).wait_recv()
        x_forward(dz, half, 3, x + 1).start()

    def x_end(dz, half):
        x_forward(dz, half, 1, x - 2).wait_recv()
        x_forward(dz, half, 3, x + 2).wait_recv()

    def l_copy(step):
        return copy(left, col * PICK, PICK, l_send.at[step - 1], l_recv.at[step - 1], at_line(step))

    def l_arrive(step):
        first = (((z_lo + 4 - step) % 4) * 2 + core) * PICK
        copy(left, first, PICK, l_send.at[step - 1], l_recv.at[step - 1], at_line(step)).wait_recv()
        copy(left, first, PICK, c_send.at[step], c_recv.at[step], sibling).start()

    def c_arrive(step):
        first = (((z_lo + 4 - step) % 4) * 2 + 1 - core) * PICK
        return copy(left, first, PICK, c_send.at[step], c_recv.at[step], sibling)

    z_copy(z_hi, 0, 1, 0).start()
    z_copy(z_hi, 1, 3, 1).start()
    z_copy(z_hi, 1, 1, 2).start()
    z_copy(z_hi, 0, 3, 3).start()
    x_start(0, 0)
    x_start(0, 1)
    copy(left, col * PICK, PICK, c_send.at[0], c_recv.at[0], sibling).start()
    x_pass(0, 0)
    x_pass(0, 1)
    z_copy(z_hi + 3, 0, 1, 0).wait_recv()
    z_copy(z_hi + 3, 0, 1, 4).start()
    z_copy(z_hi + 1, 1, 3, 1).wait_recv()
    z_copy(z_hi + 1, 1, 3, 5).start()
    x_start(3, 0)
    x_start(1, 1)
    for step in (1, 3, 2):
        l_copy(step).start()
    x_pass(3, 0)
    x_pass(1, 1)
    z_copy(z_hi + 3, 1, 1, 2).wait_recv()
    x_start(3, 1)
    z_copy(z_hi + 1, 0, 3, 3).wait_recv()
    x_start(1, 0)
    x_pass(3, 1)
    x_pass(1, 0)
    z_copy(z_hi + 2, 0, 1, 4).wait_recv()
    x_start(2, 0)
    z_copy(z_hi + 2, 1, 3, 5).wait_recv()
    x_start(2, 1)
    x_pass(2, 0)
    x_pass(2, 1)
    for step in (1, 3, 2):
        l_arrive(step)
    for dz in (0, 3, 1, 2):
        for half in (0, 1):
            x_end(dz, half)
    for step in (0, 1, 3, 2):
        c_arrive(step).wait_recv()

    def product(s):
        count = term_count[s]
        total = None
        for t in range(0, TERMS, 2):
            ids = [jnp.where(t + i < count, term_left[s, t + i], N_LEFT) for i in range(2)]
            lhs = jnp.concatenate([left[i] for i in ids], axis=1)
            rhs = jnp.concatenate([right[term_right[s, t + i]] for i in range(2)], axis=0)
            now = jnp.dot(lhs, rhs, preferred_element_type=jnp.float32)
            total = now if total is None else total + now
        return total

    def y_copy(src, i, dst, j, k, step):
        return pltpu.make_async_remote_copy(
            src_ref=src.at[i],
            dst_ref=dst.at[j],
            send_sem=y_send.at[k],
            recv_sem=y_recv.at[k],
            device_id=at_y(step),
            device_id_type=MESH,
        )

    far = ((layer + 2) % 4) * PICK
    up = ((layer + 1) % 4) * PICK
    down = ((layer + 3) % 4) * PICK
    own = layer * PICK

    def far_up(j):
        return y_copy(part, far + j, from_down, j, j, 1)

    def far_down(j):
        return y_copy(part, far + 2 + j, from_up, j, 2 + j, 3)

    def near_up(j):
        return y_copy(part, up + j, last_down, j, 4 + j, 1)

    def near_down(j):
        return y_copy(part, down + j, last_up, j, 8 + j, 3)

    @pl.loop(0, 2)
    def _(j):
        part[far + j] = product(far + j)
        far_up(j).start()
        part[far + 2 + j] = product(far + 2 + j)
        far_down(j).start()

    @pl.loop(0, 2)
    def _(j):
        part[up + 2 + j] = product(up + 2 + j)
        near_up(2 + j).start()
        part[down + j] = product(down + j)
        near_down(j).start()

    @pl.loop(0, 2)
    def _(j):
        one = product(up + j)
        far_up(j).wait_recv()
        part[up + j] = one + from_down[j]
        near_up(j).start()
        two = product(down + 2 + j)
        far_down(j).wait_recv()
        part[down + 2 + j] = two + from_up[j]
        near_down(2 + j).start()

    @pl.loop(0, PICK)
    def _(j):
        part[own + j] = product(own + j)

    for j in (2, 3, 0, 1):
        near_up(j).wait_recv()
        near_down((j + 2) % 4).wait_recv()
    for j in range(PICK):
        out[j] = part[own + j] + last_down[j] + last_up[j]

    z_copy(z_hi, 0, 1, 0).wait_send()
    z_copy(z_hi, 1, 3, 1).wait_send()
    z_copy(z_hi, 1, 1, 2).wait_send()
    z_copy(z_hi, 0, 3, 3).wait_send()
    z_copy(z_hi + 3, 0, 1, 4).wait_send()
    z_copy(z_hi + 1, 1, 3, 5).wait_send()
    for dz in range(4):
        for half in range(2):
            for step in (1, 3):
                x_copy(dz, half, step, x).wait_send()
                x_forward(dz, half, step, x - 2 + step).wait_send()
    for step in (1, 2, 3):
        l_copy(step).wait_send()
    for step in range(4):
        c_arrive(step).wait_send()
    for j in range(2):
        far_up(j).wait_send()
        far_down(j).wait_send()
    for j in range(PICK):
        near_up(j).wait_send()
        near_down(j).wait_send()


def shards(blocks, left_pick, right_pick, term_left, term_right, term_count):
    smem = pl.BlockSpec(memory_space=pltpu.SMEM)
    vmem = pl.BlockSpec(memory_space=pltpu.VMEM)
    dma = pltpu.SemaphoreType.DMA
    return pl.pallas_call(
        kernel,
        out_shape=jax.ShapeDtypeStruct((PICK, BS, BS), jnp.float32),
        in_specs=[vmem] + [smem] * 5,
        out_specs=vmem,
        scratch_shapes=[
            pltpu.VMEM((N_LEFT + 1, BS, BS), jnp.bfloat16),
            pltpu.VMEM((N_RIGHT, BS, BS), jnp.bfloat16),
            pltpu.VMEM((SLOTS, BS, BS), jnp.float32),
            pltpu.VMEM((2, BS, BS), jnp.float32),
            pltpu.VMEM((2, BS, BS), jnp.float32),
            pltpu.VMEM((PICK, BS, BS), jnp.float32),
            pltpu.VMEM((PICK, BS, BS), jnp.float32),
            dma((6,)),
            dma((6,)),
            dma((32,)),
            dma((32,)),
            dma((3,)),
            dma((3,)),
            dma((4,)),
            dma((4,)),
            dma((12,)),
            dma((12,)),
        ],
        compiler_params=pltpu.CompilerParams(
            collective_id=0, has_side_effects=True, vmem_limit_bytes=32 * 1024 * 1024
        ),
    )(blocks, left_pick, right_pick, term_left, term_right, term_count)


def solution(mesh):
    every = ("row", "col", "layer")
    in_specs = (P(("row", "col"), None, None), P(every), P(every), P(every, None), P(every, None), P(every))
    out_specs = P(every, None, None)
    return jax.shard_map(shards, mesh=mesh, in_specs=in_specs, out_specs=out_specs, check_vma=False)
```

time: 379 us -> 63.8 us (0.17)
  waiting for transfers between devices: 269 us -> 0 us
  Pallas kernels: 0 us -> 58.4 us
  local copies, waits for them, and re-layouts: 47.7 us -> 5.1 us
  blocking collectives: 31.7 us -> 0 us
  matrix products: 14.5 us -> 0 us
  between operations: 14.3 us -> 0.02 us
    all_gather x2 -> x0, waiting for transfers between devices: 241 us -> none  [the longest x1 220 us: shards(): col_blocks = lax.all_gather(blocks, 'row', axis=0, tiled=True)]
    pallas_call x0 -> x1, Pallas kernels: none -> 58.4 us  [shards(): pl.pallas_call(kernel, out_shape=jax.ShapeDtypeStruct((PICK, BS, BS), jnp...]
    gather x10 -> x0, local copies, waits for them, and re-layouts: 43 us -> none  [the longest x4 19.5 us: one_group(): row_blocks[left_ids]]
    unnamed x2 -> x0, blocking collectives: 31.7 us -> none
    reduce_scatter x1 -> x0, waiting for transfers between devices: 26 us -> none  [shards(): lax.psum_scatter(partial_sums, 'layer', scatter_dimension=0, tiled=True)]
    dot_general x4 -> x0, matrix products: 14.5 us -> none  [one_group(): lax.dot_general(left_sel, right_sel, (((1, 3), (1, 2)), ((0,), (0,))), pr...]
  transfers between devices with their start and end apart: 3 -> 0, of which waited for: 3 -> 0; matrix products, arithmetic and copies ran while one was open for 3% -> 0% of each run, Pallas kernels for 0% -> 0%
where the time goes in v1:
time: 63.8 us; the launch traced here: 63.5 us
  Pallas kernels  58.4 us (92%)
  local copies, waits for them, and re-layouts  5.1 us (8%)
    pallas_call x1, Pallas kernels, shards(): pl.pallas_call(kernel, out_shape=jax.ShapeDtypeStruct((PICK, BS, BS), jnp...  58.4 us
    unnamed x13, local copies, waits for them, and re-layouts  5.1 us

profile of v1, /device:TPU:1, one launch (start us, length us, event | category | flops | bytes accessed | tf_op | source)
XLA Modules:
  0.0 63.5 jit_solution(12024864899159719038)
XLA Ops:
  0.0 0.0 copy-start
  0.0 1.0 %copy-done = bf16[16,128,128]{2,1,0:T(8,128)(2,1)S(1)} copy-done((bf16[16,128,128]{2,1,0:T(8,128)(2,1)S(1)}, bf16[16,128,128]{2,1,0:T(8,128)(2,1)}, u32[]{:S(2)}) %copy-start) | copy-done | bytes 524312
  1.0 0.0 copy-start.1
  1.0 0.7 %copy-done.1 = s32[16,24]{1,0:T(8,128)S(1)} copy-done((s32[16,24]{1,0:T(8,128)S(1)}, s32[16,24]{1,0:T(8,128)}, u32[]{:S(2)}) %copy-start.1) | copy-done | bytes 1560
  1.7 0.0 copy-start.2
  1.7 0.7 %copy-done.2 = s32[16,24]{1,0:T(8,128)S(1)} copy-done((s32[16,24]{1,0:T(8,128)S(1)}, s32[16,24]{1,0:T(8,128)}, u32[]{:S(2)}) %copy-start.2) | copy-done | bytes 1560
  2.4 0.0 copy-start.3
  2.4 0.7 %copy-done.3 = s32[4]{0:T(128)S(1)} copy-done((s32[4]{0:T(128)S(1)}, s32[4]{0:T(128)}, u32[]{:S(2)}) %copy-start.3) | copy-done | bytes 40
  3.1 0.0 copy-start.4
  3.1 0.7 %copy-done.4 = s32[4]{0:T(128)S(1)} copy-done((s32[4]{0:T(128)S(1)}, s32[4]{0:T(128)}, u32[]{:S(2)}) %copy-start.4) | copy-done | bytes 40
  3.7 0.0 copy-start.5
  3.8 0.7 %copy-done.5 = s32[16]{0:T(128)S(1)} copy-done((s32[16]{0:T(128)S(1)}, s32[16]{0:T(128)}, u32[]{:S(2)}) %copy-start.5) | copy-done | bytes 88
  4.4 58.4 %shard_map.64 = f32[4,128,128]{2,1,0:T(8,128)S(1)} custom-call(bf16[16,128,128]{2,1,0:T(8,128)(2,1)S(1)} %copy-done, s32[4]{0:T(128)S(1)} %copy-done.3, s32[4]{0:T(128)S(1)} %copy-done.4, s32[16,24]{1,0:T(8,128)S(1)} %copy-done.1, s32[16,24]{1,0:T(8,128)S(1)} %copy-done.2, s32[16]{0:T(128)S(1)} %copy-done.5), custom_call_target="tpu_custom_call" | custom-call | tf_op jit(solution)/shard_map/pallas_call | solution.py:269
  62.8 0.7 %copy.8 = f32[4,128,128]{2,1,0:T(8,128)} copy(f32[4,128,128]{2,1,0:T(8,128)S(1)} %shard_map.64) | data formatting | bytes 524288
Async XLA Ops:
  0.0 1.0 %copy-start = (bf16[16,128,128]{2,1,0:T(8,128)(2,1)S(1)}, bf16[16,128,128]{2,1,0:T(8,128)(2,1)}, u32[]{:S(2)}) copy-start(bf16[16,128,128]{2,1,0:T(8,128)(2,1)} %blocks.1) | copy-start | bytes 1572868
  1.0 0.7 %copy-start.1 = (s32[16,24]{1,0:T(8,128)S(1)}, s32[16,24]{1,0:T(8,128)}, u32[]{:S(2)}) copy-start(s32[16,24]{1,0:T(8,128)} %term_left.1) | copy-start | bytes 4612
  1.7 0.7 %copy-start.2 = (s32[16,24]{1,0:T(8,128)S(1)}, s32[16,24]{1,0:T(8,128)}, u32[]{:S(2)}) copy-start(s32[16,24]{1,0:T(8,128)} %term_right.1) | copy-start | bytes 4612
  2.4 0.7 %copy-start.3 = (s32[4]{0:T(128)S(1)}, s32[4]{0:T(128)}, u32[]{:S(2)}) copy-start(s32[4]{0:T(128)} %left_pick.1) | copy-start | bytes 52
  3.1 0.7 %copy-start.4 = (s32[4]{0:T(128)S(1)}, s32[4]{0:T(128)}, u32[]{:S(2)}) copy-start(s32[4]{0:T(128)} %right_pick.1) | copy-start | bytes 52
  3.7 0.7 %copy-start.5 = (s32[16]{0:T(128)S(1)}, s32[16]{0:T(128)}, u32[]{:S(2)}) copy-start(s32[16]{0:T(128)} %term_count.1) | copy-start | bytes 196

commit v2 on v1

--- a/solution.py
+++ b/solution.py
@@ -20,13 +20,20 @@
 
 
 def kernel(
+    blocks_in,
+    left_pick_in,
+    right_pick_in,
+    term_left_in,
+    term_right_in,
+    term_count_in,
+    out,
     blocks,
     left_pick,
     right_pick,
     term_left,
     term_right,
     term_count,
-    out,
+    in_sem,
     left,
     right,
     part,
@@ -65,16 +72,39 @@
 
     sibling = (row, z_lo * 2 + 1 - core, layer)
 
+    pairs = [
+        (left_pick_in, left_pick),
+        (right_pick_in, right_pick),
+        (blocks_in, blocks),
+        (term_left_in, term_left),
+        (term_right_in, term_right),
+        (term_count_in, term_count),
+    ]
+    loads = [pltpu.make_async_copy(src, dst, in_sem.at[i]) for i, (src, dst) in enumerate(pairs)]
+    for load in loads:
+        load.start()
     barrier = pltpu.get_barrier_semaphore()
-    partners = [at_z(1), at_z(3), at_x(1), at_x(3), at_line(1), at_line(2), at_line(3), sibling, at_y(1), at_y(3)]
+    partners = [at_z(1), at_z(3), at_x(1), at_x(3), sibling, at_y(1), at_y(3)]
     for partner in partners:
         pl.semaphore_signal(barrier, inc=1, device_id=partner, device_id_type=MESH)
+
+    @pl.when(z_lo < 3)
+    def _():
+        pl.semaphore_signal(barrier, inc=1, device_id=at_line(1), device_id_type=MESH)
+
+    @pl.when(z_lo > 0)
+    def _():
+        pl.semaphore_signal(barrier, inc=1, device_id=at_line(3), device_id_type=MESH)
+
+    for load in loads[:3]:
+        load.wait()
     for j in range(PICK):
         right[row * PICK + j] = blocks[right_pick[j]]
     for j in range(PICK):
         left[col * PICK + j] = blocks[left_pick[j]]
     left[N_LEFT] = jnp.zeros((BS, BS), jnp.bfloat16)
-    pl.semaphore_wait(barrier, len(partners))
+    inner = jnp.where((z_lo > 0) & (z_lo < 3), 1, 0)
+    pl.semaphore_wait(barrier, len(partners) + 1 + inner)
 
     def copy(ref, first, count, send, recv, target):
         return pltpu.make_async_remote_copy(
@@ -115,56 +145,94 @@
         x_forward(dz, half, 1, x - 2).wait_recv()
         x_forward(dz, half, 3, x + 2).wait_recv()
 
-    def l_copy(step):
-        return copy(left, col * PICK, PICK, l_send.at[step - 1], l_recv.at[step - 1], at_line(step))
-
-    def l_arrive(step):
-        first = (((z_lo + 4 - step) % 4) * 2 + core) * PICK
-        copy(left, first, PICK, l_send.at[step - 1], l_recv.at[step - 1], at_line(step)).wait_recv()
-        copy(left, first, PICK, c_send.at[step], c_recv.at[step], sibling).start()
-
-    def c_arrive(step):
-        first = (((z_lo + 4 - step) % 4) * 2 + 1 - core) * PICK
-        return copy(left, first, PICK, c_send.at[step], c_recv.at[step], sibling)
+    def l_copy(place, step):
+        k = 2 * place + (0 if step == 1 else 1)
+        return copy(left, (place * 2 + core) * PICK, PICK, l_send.at[k], l_recv.at[place], at_line(step))
+
+    def l_start():
+        @pl.when(z_lo < 3)
+        def _():
+            l_copy(z_lo, 1).start()
+
+        @pl.when(z_lo > 0)
+        def _():
+            l_copy(z_lo, 3).start()
+
+    def c_copy(place, side):
+        return copy(left, (place * 2 + side) * PICK, PICK, c_send.at[place], c_recv.at[place], sibling)
+
+    def l_pass(distance):
+        @pl.when(z_lo >= distance)
+        def _():
+            place = z_lo - distance
+            l_copy(place, 1).wait_recv()
+
+            @pl.when(z_lo < 3)
+            def _():
+                l_copy(place, 1).start()
+
+            c_copy(place, core).start()
+
+        @pl.when(z_lo + distance <= 3)
+        def _():
+            place = z_lo + distance
+            l_copy(place, 3).wait_recv()
+
+            @pl.when(z_lo > 0)
+            def _():
+                l_copy(place, 3).start()
+
+            c_copy(place, core).start()
 
     z_copy(z_hi, 0, 1, 0).start()
     z_copy(z_hi, 1, 3, 1).start()
-    z_copy(z_hi, 1, 1, 2).start()
-    z_copy(z_hi, 0, 3, 3).start()
     x_start(0, 0)
     x_start(0, 1)
-    copy(left, col * PICK, PICK, c_send.at[0], c_recv.at[0], sibling).start()
+    c_copy(z_lo, core).start()
     x_pass(0, 0)
     x_pass(0, 1)
+    z_copy(z_hi, 0, 1, 0).wait_send()
+    z_copy(z_hi, 1, 1, 2).start()
+    z_copy(z_hi, 1, 3, 1).wait_send()
+    z_copy(z_hi, 0, 3, 3).start()
+    l_start()
     z_copy(z_hi + 3, 0, 1, 0).wait_recv()
-    z_copy(z_hi + 3, 0, 1, 4).start()
+    x_start(3, 0)
     z_copy(z_hi + 1, 1, 3, 1).wait_recv()
-    z_copy(z_hi + 1, 1, 3, 5).start()
-    x_start(3, 0)
     x_start(1, 1)
-    for step in (1, 3, 2):
-        l_copy(step).start()
     x_pass(3, 0)
     x_pass(1, 1)
+    z_copy(z_hi, 1, 1, 2).wait_send()
+    z_copy(z_hi + 3, 0, 1, 4).start()
+    z_copy(z_hi, 0, 3, 3).wait_send()
+    z_copy(z_hi + 1, 1, 3, 5).start()
     z_copy(z_hi + 3, 1, 1, 2).wait_recv()
     x_start(3, 1)
     z_copy(z_hi + 1, 0, 3, 3).wait_recv()
     x_start(1, 0)
+    l_pass(1)
     x_pass(3, 1)
     x_pass(1, 0)
     z_copy(z_hi + 2, 0, 1, 4).wait_recv()
     x_start(2, 0)
     z_copy(z_hi + 2, 1, 3, 5).wait_recv()
     x_start(2, 1)
+    l_pass(2)
     x_pass(2, 0)
     x_pass(2, 1)
-    for step in (1, 3, 2):
-        l_arrive(step)
-    for dz in (0, 3, 1, 2):
-        for half in (0, 1):
-            x_end(dz, half)
-    for step in (0, 1, 3, 2):
-        c_arrive(step).wait_recv()
+    l_pass(3)
+    x_end(0, 0)
+    x_end(0, 1)
+    x_end(3, 0)
+    x_end(1, 1)
+    x_end(3, 1)
+    x_end(1, 0)
+    x_end(2, 0)
+    x_end(2, 1)
+    for place in range(4):
+        c_copy(place, 1 - core).wait_recv()
+    for load in loads[3:]:
+        load.wait()
 
     def product(s):
         count = term_count[s]
@@ -239,10 +307,6 @@
     for j in range(PICK):
         out[j] = part[own + j] + last_down[j] + last_up[j]
 
-    z_copy(z_hi, 0, 1, 0).wait_send()
-    z_copy(z_hi, 1, 3, 1).wait_send()
-    z_copy(z_hi, 1, 1, 2).wait_send()
-    z_copy(z_hi, 0, 3, 3).wait_send()
     z_copy(z_hi + 3, 0, 1, 4).wait_send()
     z_copy(z_hi + 1, 1, 3, 5).wait_send()
     for dz in range(4):
@@ -250,10 +314,17 @@
             for step in (1, 3):
                 x_copy(dz, half, step, x).wait_send()
                 x_forward(dz, half, step, x - 2 + step).wait_send()
-    for step in (1, 2, 3):
-        l_copy(step).wait_send()
-    for step in range(4):
-        c_arrive(step).wait_send()
+    for place in range(4):
+
+        @pl.when((place <= z_lo) & (z_lo < 3))
+        def _():
+            l_copy(place, 1).wait_send()
+
+        @pl.when((place >= z_lo) & (z_lo > 0))
+        def _():
+            l_copy(place, 3).wait_send()
+
+        c_copy(place, core).wait_send()
     for j in range(2):
         far_up(j).wait_send()
         far_down(j).wait_send()
@@ -262,16 +333,22 @@
         near_down(j).wait_send()
 
 
-def shards(blocks, left_pick, right_pick, term_left, term_right, term_count):
-    smem = pl.BlockSpec(memory_space=pltpu.SMEM)
+def shards(*arrays):
     vmem = pl.BlockSpec(memory_space=pltpu.VMEM)
     dma = pltpu.SemaphoreType.DMA
     return pl.pallas_call(
         kernel,
         out_shape=jax.ShapeDtypeStruct((PICK, BS, BS), jnp.float32),
-        in_specs=[vmem] + [smem] * 5,
+        in_specs=[pl.BlockSpec(memory_space=pl.ANY)] * 6,
         out_specs=vmem,
         scratch_shapes=[
+            pltpu.VMEM((SLOTS, BS, BS), jnp.bfloat16),
+            pltpu.SMEM((PICK,), jnp.int32),
+            pltpu.SMEM((PICK,), jnp.int32),
+            pltpu.SMEM((SLOTS, TERMS), jnp.int32),
+            pltpu.SMEM((SLOTS, TERMS), jnp.int32),
+            pltpu.SMEM((SLOTS,), jnp.int32),
+            dma((6,)),
             pltpu.VMEM((N_LEFT + 1, BS, BS), jnp.bfloat16),
             pltpu.VMEM((N_RIGHT, BS, BS), jnp.bfloat16),
             pltpu.VMEM((SLOTS, BS, BS), jnp.float32),
@@ -283,8 +360,8 @@
             dma((6,)),
             dma((32,)),
             dma((32,)),
-            dma((3,)),
-            dma((3,)),
+            dma((8,)),
+            dma((4,)),
             dma((4,)),
             dma((4,)),
             dma((12,)),
@@ -293,7 +370,7 @@
         compiler_params=pltpu.CompilerParams(
             collective_id=0, has_side_effects=True, vmem_limit_bytes=32 * 1024 * 1024
         ),
-    )(blocks, left_pick, right_pick, term_left, term_right, term_count)
+    )(*[pltpu.with_memory_space_constraint(a, pltpu.HBM) for a in arrays])
 
 
 def solution(mesh):

time: 63.8 us -> 55.8 us (0.87)
  local copies, waits for them, and re-layouts: 5.1 us -> 0.71 us
  Pallas kernels: 58.4 us -> 54.5 us
    unnamed x13 -> x1, local copies, waits for them, and re-layouts: 5.1 us -> 0.71 us
    pallas_call x1, Pallas kernels: 58.4 us -> 54.5 us  [shards(): pl.pallas_call(kernel, out_shape=jax.ShapeDtypeStruct((PICK, BS, BS), jnp...]
where the time goes in v2:
time: 55.8 us; the launch traced here: 55.2 us
  Pallas kernels  54.5 us (98%)
  local copies, waits for them, and re-layouts  0.71 us (1%)
    pallas_call x1, Pallas kernels, shards(): pl.pallas_call(kernel, out_shape=jax.ShapeDtypeStruct((PICK, BS, BS), jnp...  54.5 us

profile of v2, /device:TPU:1, one launch (start us, length us, event | category | flops | bytes accessed | tf_op | source)
XLA Modules:
  0.0 55.2 jit_solution(7780756990591785563)
XLA Ops:
  0.0 54.5 %shard_map.64 = f32[4,128,128]{2,1,0:T(8,128)S(1)} custom-call(bf16[16,128,128]{2,1,0:T(8,128)(2,1)} %blocks_in.1, s32[4]{0:T(128)} %left_pick_in.1, s32[4]{0:T(128)} %right_pick_in.1, s32[16,24]{1,0:T(8,128)} %term_left_in.1, s32[16,24]{1,0:T(8,128)} %term_right_in.1, s32[16]{0:T(128)} %term_count_in.1), custom_call_target="tpu_custom_call" | custom-call | tf_op jit(solution)/shard_map/pallas_call | solution.py:339
  54.5 0.7 %copy.8 = f32[4,128,128]{2,1,0:T(8,128)} copy(f32[4,128,128]{2,1,0:T(8,128)S(1)} %shard_map.64) | data formatting | bytes 524288

commit v3 on v2

--- a/solution.py
+++ b/solution.py
@@ -12,6 +12,8 @@
 PICK = 4
 SLOTS = 16
 TERMS = 24
+LEVELS = 32760.0
+EXTRA = 16
 N_ROW = 16
 N_COL = 8
 N_LAYER = 4
@@ -37,10 +39,8 @@
     left,
     right,
     part,
-    from_down,
-    from_up,
-    last_down,
-    last_up,
+    packed,
+    arrived,
     z_send,
     z_recv,
     x_send,
@@ -84,7 +84,7 @@
     for load in loads:
         load.start()
     barrier = pltpu.get_barrier_semaphore()
-    partners = [at_z(1), at_z(3), at_x(1), at_x(3), sibling, at_y(1), at_y(3)]
+    partners = [at_z(1), at_z(3), at_x(1), at_x(2), at_x(3), sibling, at_y(1), at_y(2), at_y(3)]
     for partner in partners:
         pl.semaphore_signal(barrier, inc=1, device_id=partner, device_id_type=MESH)
 
@@ -123,27 +123,16 @@
         return copy(right, first_of(h, x, half), 2, z_send.at[k], z_recv.at[k], at_z(step))
 
     def x_copy(dz, half, step, xx):
-        k = (dz * 2 + half) * 2 + (0 if step == 1 else 1)
+        k = (dz * 2 + half) * 3 + step - 1
         return copy(right, first_of(z_hi + dz, xx, half), 2, x_send.at[k], x_recv.at[k], at_x(step))
 
-    def x_forward(dz, half, step, xx):
-        k = 16 + (dz * 2 + half) * 2 + (0 if step == 1 else 1)
-        piece = 0 if step == 1 else 1
-        return copy(right, first_of(z_hi + dz, xx, half) + piece, 1, x_send.at[k], x_recv.at[k], at_x(step))
-
     def x_start(dz, half):
-        x_copy(dz, half, 1, x).start()
-        x_copy(dz, half, 3, x).start()
-
-    def x_pass(dz, half):
-        x_copy(dz, half, 1, x - 1).wait_recv()
-        x_forward(dz, half, 1, x - 1).start()
-        x_copy(dz, half, 3, x + 1).wait_recv()
-        x_forward(dz, half, 3, x + 1).start()
+        for step in (1, 3, 2):
+            x_copy(dz, half, step, x).start()
 
     def x_end(dz, half):
-        x_forward(dz, half, 1, x - 2).wait_recv()
-        x_forward(dz, half, 3, x + 2).wait_recv()
+        for step in (1, 3, 2):
+            x_copy(dz, half, step, x - step).wait_recv()
 
     def l_copy(place, step):
         k = 2 * place + (0 if step == 1 else 1)
@@ -189,8 +178,6 @@
     x_start(0, 0)
     x_start(0, 1)
     c_copy(z_lo, core).start()
-    x_pass(0, 0)
-    x_pass(0, 1)
     z_copy(z_hi, 0, 1, 0).wait_send()
     z_copy(z_hi, 1, 1, 2).start()
     z_copy(z_hi, 1, 3, 1).wait_send()
@@ -200,8 +187,6 @@
     x_start(3, 0)
     z_copy(z_hi + 1, 1, 3, 1).wait_recv()
     x_start(1, 1)
-    x_pass(3, 0)
-    x_pass(1, 1)
     z_copy(z_hi, 1, 1, 2).wait_send()
     z_copy(z_hi + 3, 0, 1, 4).start()
     z_copy(z_hi, 0, 3, 3).wait_send()
@@ -211,24 +196,15 @@
     z_copy(z_hi + 1, 0, 3, 3).wait_recv()
     x_start(1, 0)
     l_pass(1)
-    x_pass(3, 1)
-    x_pass(1, 0)
     z_copy(z_hi + 2, 0, 1, 4).wait_recv()
     x_start(2, 0)
+    l_pass(2)
     z_copy(z_hi + 2, 1, 3, 5).wait_recv()
     x_start(2, 1)
-    l_pass(2)
-    x_pass(2, 0)
-    x_pass(2, 1)
     l_pass(3)
-    x_end(0, 0)
-    x_end(0, 1)
-    x_end(3, 0)
-    x_end(1, 1)
-    x_end(3, 1)
-    x_end(1, 0)
-    x_end(2, 0)
-    x_end(2, 1)
+    for dz in (0, 3, 1, 2):
+        for half in range(2):
+            x_end(dz, half)
     for place in range(4):
         c_copy(place, 1 - core).wait_recv()
     for load in loads[3:]:
@@ -245,9 +221,24 @@
             total = now if total is None else total + now
         return total
 
-    def y_copy(src, i, dst, j, k, step):
+    def code(value):
+        top = jnp.max(jnp.abs(value), axis=0, keepdims=True)
+        power = jnp.clip(jnp.ceil(jnp.log2(top)), -120.0, 120.0)
+        digits = jnp.floor(value * (jnp.exp2(-power) * LEVELS) + 0.5)
+        return digits.astype(jnp.int32).astype(jnp.int16), jnp.broadcast_to(power, (EXTRA, BS)).astype(jnp.int32).astype(jnp.int16)
+
+    def put(j, value):
+        digits, power = code(value)
+        packed[j, pl.ds(0, BS)] = digits
+        packed[j, pl.ds(BS, EXTRA)] = power
+
+    def get(ref, j):
+        power = ref[j, pl.ds(BS, EXTRA)].astype(jnp.int32).astype(jnp.float32)[0:1]
+        return ref[j, pl.ds(0, BS)].astype(jnp.int32).astype(jnp.float32) * (jnp.exp2(power) * (1.0 / LEVELS))
+
+    def y_copy(i, dst, j, k, step):
         return pltpu.make_async_remote_copy(
-            src_ref=src.at[i],
+            src_ref=packed.at[i],
             dst_ref=dst.at[j],
             send_sem=y_send.at[k],
             recv_sem=y_recv.at[k],
@@ -255,65 +246,36 @@
             device_id_type=MESH,
         )
 
-    far = ((layer + 2) % 4) * PICK
-    up = ((layer + 1) % 4) * PICK
-    down = ((layer + 3) % 4) * PICK
-    own = layer * PICK
-
-    def far_up(j):
-        return y_copy(part, far + j, from_down, j, j, 1)
-
-    def far_down(j):
-        return y_copy(part, far + 2 + j, from_up, j, 2 + j, 3)
-
-    def near_up(j):
-        return y_copy(part, up + j, last_down, j, 4 + j, 1)
-
-    def near_down(j):
-        return y_copy(part, down + j, last_up, j, 8 + j, 3)
-
-    @pl.loop(0, 2)
-    def _(j):
-        part[far + j] = product(far + j)
-        far_up(j).start()
-        part[far + 2 + j] = product(far + 2 + j)
-        far_down(j).start()
-
-    @pl.loop(0, 2)
-    def _(j):
-        part[up + 2 + j] = product(up + 2 + j)
-        near_up(2 + j).start()
-        part[down + j] = product(down + j)
-        near_down(j).start()
-
-    @pl.loop(0, 2)
-    def _(j):
-        one = product(up + j)
-        far_up(j).wait_recv()
-        part[up + j] = one + from_down[j]
-        near_up(j).start()
-        two = product(down + 2 + j)
-        far_down(j).wait_recv()
-        part[down + 2 + j] = two + from_up[j]
-        near_down(2 + j).start()
-
-    @pl.loop(0, PICK)
-    def _(j):
-        part[own + j] = product(own + j)
-
-    for j in (2, 3, 0, 1):
-        near_up(j).wait_recv()
-        near_down((j + 2) % 4).wait_recv()
+    def sent(step, j):
+        return y_copy((step - 1) * PICK + j, arrived, (step - 1) * PICK + j, (step - 1) * PICK + j, step)
+
+    def send(step, picks):
+        first = ((layer + step) % 4) * PICK
+        for j, value in [(j, product(first + j)) for j in picks]:
+            put((step - 1) * PICK + j, value)
+        for j in picks:
+            sent(step, j).start()
+
+    send(2, (0, 1))
+    send(2, (2, 3))
+    send(1, (0, 1, 2, 3))
+    send(3, (0, 1, 2, 3))
     for j in range(PICK):
-        out[j] = part[own + j] + last_down[j] + last_up[j]
+        part[j] = product(layer * PICK + j)
+
+    for j in range(PICK):
+        total = part[j]
+        for step in (2, 1, 3):
+            sent(step, j).wait_recv()
+            total += get(arrived, (step - 1) * PICK + j)
+        out[j] = total
 
     z_copy(z_hi + 3, 0, 1, 4).wait_send()
     z_copy(z_hi + 1, 1, 3, 5).wait_send()
     for dz in range(4):
         for half in range(2):
-            for step in (1, 3):
+            for step in (1, 2, 3):
                 x_copy(dz, half, step, x).wait_send()
-                x_forward(dz, half, step, x - 2 + step).wait_send()
     for place in range(4):
 
         @pl.when((place <= z_lo) & (z_lo < 3))
@@ -325,12 +287,9 @@
             l_copy(place, 3).wait_send()
 
         c_copy(place, core).wait_send()
-    for j in range(2):
-        far_up(j).wait_send()
-        far_down(j).wait_send()
-    for j in range(PICK):
-        near_up(j).wait_send()
-        near_down(j).wait_send()
+    for step in (1, 2, 3):
+        for j in range(PICK):
+            sent(step, j).wait_send()
 
 
 def shards(*arrays):
@@ -351,15 +310,13 @@
             dma((6,)),
             pltpu.VMEM((N_LEFT + 1, BS, BS), jnp.bfloat16),
             pltpu.VMEM((N_RIGHT, BS, BS), jnp.bfloat16),
-            pltpu.VMEM((SLOTS, BS, BS), jnp.float32),
-            pltpu.VMEM((2, BS, BS), jnp.float32),
-            pltpu.VMEM((2, BS, BS), jnp.float32),
             pltpu.VMEM((PICK, BS, BS), jnp.float32),
-            pltpu.VMEM((PICK, BS, BS), jnp.float32),
+            pltpu.VMEM((3 * PICK, BS + EXTRA, BS), jnp.int16),
+            pltpu.VMEM((3 * PICK, BS + EXTRA, BS), jnp.int16),
             dma((6,)),
             dma((6,)),
-            dma((32,)),
-            dma((32,)),
+            dma((24,)),
+            dma((24,)),
             dma((8,)),
             dma((4,)),
             dma((4,)),

time: 55.8 us -> 54 us (0.968)
  the two profiles are of different devices: /device:TPU:1 before, /device:TPU:7 now
where the time goes in v3:
time: 54 us; the launch traced here: 53.9 us
  Pallas kernels  53.2 us (99%)
  local copies, waits for them, and re-layouts  0.71 us (1%)
    pallas_call x1, Pallas kernels, shards(): pl.pallas_call(kernel, out_shape=jax.ShapeDtypeStruct((PICK, BS, BS), jnp...  53.2 us

profile of v3, /device:TPU:7, one launch (start us, length us, event | category | flops | bytes accessed | tf_op | source)
XLA Modules:
  0.0 53.9 jit_solution(8746894720155084083)
XLA Ops:
  0.0 53.2 %shard_map.64 = f32[4,128,128]{2,1,0:T(8,128)S(1)} custom-call(bf16[16,128,128]{2,1,0:T(8,128)(2,1)} %blocks_in.1, s32[4]{0:T(128)} %left_pick_in.1, s32[4]{0:T(128)} %right_pick_in.1, s32[16,24]{1,0:T(8,128)} %term_left_in.1, s32[16,24]{1,0:T(8,128)} %term_right_in.1, s32[16]{0:T(128)} %term_count_in.1), custom_call_target="tpu_custom_call" | custom-call | tf_op jit(solution)/shard_map/pallas_call | solution.py:298
  53.2 0.7 %copy.8 = f32[4,128,128]{2,1,0:T(8,128)} copy(f32[4,128,128]{2,1,0:T(8,128)S(1)} %shard_map.64) | data formatting | bytes 524288

commit v4 on v3

--- a/solution.py
+++ b/solution.py
@@ -40,7 +40,10 @@
     right,
     part,
     packed,
-    arrived,
+    from_down,
+    from_up,
+    last_down,
+    last_up,
     z_send,
     z_recv,
     x_send,
@@ -84,7 +87,7 @@
     for load in loads:
         load.start()
     barrier = pltpu.get_barrier_semaphore()
-    partners = [at_z(1), at_z(3), at_x(1), at_x(2), at_x(3), sibling, at_y(1), at_y(2), at_y(3)]
+    partners = [at_z(1), at_z(3), at_x(1), at_x(2), at_x(3), sibling, at_y(1), at_y(3)]
     for partner in partners:
         pl.semaphore_signal(barrier, inc=1, device_id=partner, device_id_type=MESH)
 
@@ -246,29 +249,52 @@
             device_id_type=MESH,
         )
 
-    def sent(step, j):
-        return y_copy((step - 1) * PICK + j, arrived, (step - 1) * PICK + j, (step - 1) * PICK + j, step)
-
-    def send(step, picks):
-        first = ((layer + step) % 4) * PICK
-        for j, value in [(j, product(first + j)) for j in picks]:
-            put((step - 1) * PICK + j, value)
-        for j in picks:
-            sent(step, j).start()
-
-    send(2, (0, 1))
-    send(2, (2, 3))
-    send(1, (0, 1, 2, 3))
-    send(3, (0, 1, 2, 3))
-    for j in range(PICK):
-        part[j] = product(layer * PICK + j)
-
-    for j in range(PICK):
-        total = part[j]
-        for step in (2, 1, 3):
-            sent(step, j).wait_recv()
-            total += get(arrived, (step - 1) * PICK + j)
-        out[j] = total
+    far = ((layer + 2) % 4) * PICK
+    up = ((layer + 1) % 4) * PICK
+    down = ((layer + 3) % 4) * PICK
+    own = layer * PICK
+
+    def far_up(j):
+        return y_copy(j, from_down, j, j, 1)
+
+    def far_down(j):
+        return y_copy(2 + j, from_up, j, 2 + j, 3)
+
+    def near_up(j):
+        return y_copy(4 + j, last_down, j, 4 + j, 1)
+
+    def near_down(j):
+        return y_copy(8 + j, last_up, j, 8 + j, 3)
+
+    @pl.loop(0, 2)
+    def _(j):
+        one, two = product(far + j), product(far + 2 + j)
+        put(j, one)
+        put(2 + j, two)
+        far_up(j).start()
+        far_down(j).start()
+
+    for j in range(2):
+        put(6 + j, product(up + 2 + j))
+        put(8 + j, product(down + j))
+    for j in range(2):
+        near_up(2 + j).start()
+        near_down(j).start()
+    sums = [(product(up + j), product(down + 2 + j)) for j in range(2)]
+    for j in range(2):
+        far_up(j).wait_recv()
+        put(4 + j, sums[j][0] + get(from_down, j))
+        near_up(j).start()
+        far_down(j).wait_recv()
+        put(10 + j, sums[j][1] + get(from_up, j))
+        near_down(2 + j).start()
+    for j in range(PICK):
+        part[j] = product(own + j)
+    for j in (2, 3, 0, 1):
+        near_up(j).wait_recv()
+        near_down((j + 2) % 4).wait_recv()
+    for j in range(PICK):
+        out[j] = part[j] + get(last_down, j) + get(last_up, j)
 
     z_copy(z_hi + 3, 0, 1, 4).wait_send()
     z_copy(z_hi + 1, 1, 3, 5).wait_send()
@@ -287,9 +313,12 @@
             l_copy(place, 3).wait_send()
 
         c_copy(place, core).wait_send()
-    for step in (1, 2, 3):
-        for j in range(PICK):
-            sent(step, j).wait_send()
+    for j in range(2):
+        far_up(j).wait_send()
+        far_down(j).wait_send()
+    for j in range(PICK):
+        near_up(j).wait_send()
+        near_down(j).wait_send()
 
 
 def shards(*arrays):
@@ -312,7 +341,10 @@
             pltpu.VMEM((N_RIGHT, BS, BS), jnp.bfloat16),
             pltpu.VMEM((PICK, BS, BS), jnp.float32),
             pltpu.VMEM((3 * PICK, BS + EXTRA, BS), jnp.int16),
-            pltpu.VMEM((3 * PICK, BS + EXTRA, BS), jnp.int16),
+            pltpu.VMEM((2, BS + EXTRA, BS), jnp.int16),
+            pltpu.VMEM((2, BS + EXTRA, BS), jnp.int16),
+            pltpu.VMEM((PICK, BS + EXTRA, BS), jnp.int16),
+            pltpu.VMEM((PICK, BS + EXTRA, BS), jnp.int16),
             dma((6,)),
             dma((6,)),
             dma((24,)),

time: 54 us -> 53.4 us (0.989)
  the two profiles are of different devices: /device:TPU:7 before, /device:TPU:8 now
where the time goes in v4:
time: 53.4 us; the launch traced here: 53.2 us
  Pallas kernels  52.5 us (98%)
  local copies, waits for them, and re-layouts  0.71 us (1%)
    pallas_call x1, Pallas kernels, shards(): pl.pallas_call(kernel, out_shape=jax.ShapeDtypeStruct((PICK, BS, BS), jnp...  52.5 us

profile of v4, /device:TPU:8, one launch (start us, length us, event | category | flops | bytes accessed | tf_op | source)
XLA Modules:
  0.0 53.2 jit_solution(16837643465594641542)
XLA Ops:
  0.0 52.5 %shard_map.64 = f32[4,128,128]{2,1,0:T(8,128)S(1)} custom-call(bf16[16,128,128]{2,1,0:T(8,128)(2,1)} %blocks_in.1, s32[4]{0:T(128)} %left_pick_in.1, s32[4]{0:T(128)} %right_pick_in.1, s32[16,24]{1,0:T(8,128)} %term_left_in.1, s32[16,24]{1,0:T(8,128)} %term_right_in.1, s32[16]{0:T(128)} %term_count_in.1), custom_call_target="tpu_custom_call" | custom-call | tf_op jit(solution)/shard_map/pallas_call | solution.py:327
  52.5 0.7 %copy.8 = f32[4,128,128]{2,1,0:T(8,128)} copy(f32[4,128,128]{2,1,0:T(8,128)S(1)} %shard_map.64) | data formatting | bytes 524288

commit v5 on v4

--- a/solution.py
+++ b/solution.py
@@ -187,13 +187,11 @@
     z_copy(z_hi, 0, 3, 3).start()
     l_start()
     z_copy(z_hi + 3, 0, 1, 0).wait_recv()
+    z_copy(z_hi + 3, 0, 1, 4).start()
     x_start(3, 0)
     z_copy(z_hi + 1, 1, 3, 1).wait_recv()
+    z_copy(z_hi + 1, 1, 3, 5).start()
     x_start(1, 1)
-    z_copy(z_hi, 1, 1, 2).wait_send()
-    z_copy(z_hi + 3, 0, 1, 4).start()
-    z_copy(z_hi, 0, 3, 3).wait_send()
-    z_copy(z_hi + 1, 1, 3, 5).start()
     z_copy(z_hi + 3, 1, 1, 2).wait_recv()
     x_start(3, 1)
     z_copy(z_hi + 1, 0, 3, 3).wait_recv()
@@ -296,6 +294,8 @@
     for j in range(PICK):
         out[j] = part[j] + get(last_down, j) + get(last_up, j)
 
+    z_copy(z_hi, 1, 1, 2).wait_send()
+    z_copy(z_hi, 0, 3, 3).wait_send()
     z_copy(z_hi + 3, 0, 1, 4).wait_send()
     z_copy(z_hi + 1, 1, 3, 5).wait_send()
     for dz in range(4):

time: 53.4 us -> 53.4 us (level)
  no operation moved by 1% of the time
where the time goes in v5:
time: 53.4 us; the launch traced here: 53.3 us
  Pallas kernels  52.5 us (98%)
  local copies, waits for them, and re-layouts  0.71 us (1%)
    pallas_call x1, Pallas kernels, shards(): pl.pallas_call(kernel, out_shape=jax.ShapeDtypeStruct((PICK, BS, BS), jnp...  52.5 us

profile of v5, /device:TPU:8, one launch (start us, length us, event | category | flops | bytes accessed | tf_op | source)
XLA Modules:
  0.0 53.3 jit_solution(13872675578087199168)
XLA Ops:
  0.0 52.5 %shard_map.64 = f32[4,128,128]{2,1,0:T(8,128)S(1)} custom-call(bf16[16,128,128]{2,1,0:T(8,128)(2,1)} %blocks_in.1, s32[4]{0:T(128)} %left_pick_in.1, s32[4]{0:T(128)} %right_pick_in.1, s32[16,24]{1,0:T(8,128)} %term_left_in.1, s32[16,24]{1,0:T(8,128)} %term_right_in.1, s32[16]{0:T(128)} %term_count_in.1), custom_call_target="tpu_custom_call" | custom-call | tf_op jit(solution)/shard_map/pallas_call | solution.py:327
  52.6 0.7 %copy.8 = f32[4,128,128]{2,1,0:T(8,128)} copy(f32[4,128,128]{2,1,0:T(8,128)S(1)} %shard_map.64) | data formatting | bytes 524288
